TPU v7x, 128 devices: a whole 4x4x4 slice. The times are simulated.
128 devices in a mesh: enc: 8 (over y, core), seq: 16 (over x, z).
Axes of the slice: x: 4, y: 4, z: 4, core: 2. Of those that a mesh axis runs over, the one named last changes fastest.
Arguments:
- frame_tiles: bfloat16 [8, 16, 2, 16, 32, 768], P('enc', 'seq'), may hold values from -6 to 6
- tile_ids: int32 [8, 16, 2], P('enc', 'seq'), may hold values from 0 to 15, as said below
- partner_slot: int32 [8, 16, 2], P('enc', 'seq'), may hold values from 0 to 15, as said below
- mix_kernel: bfloat16 [7, 7, 768], replicated, may hold values from -0.875 to 0.875
- mix_bias: float32 [768], replicated, may hold values from -3 to 3
- down_weight: bfloat16 [3072, 1536], replicated, may hold values from -0.109375 to 0.109375
- down_bias: float32 [1536], replicated, may hold values from -3 to 3
- token_pos: int32 [8, 16, 2, 128], P('enc', 'seq'), may hold values from 0 to 32767, as said below
- grad_rows: bfloat16 [32768, 1536], P(('enc', 'seq')), may hold values from -6 to 6
Outputs:
- llm_rows: bfloat16 [32768, 1536], P(('enc', 'seq'))
- grad_tiles: bfloat16 [8, 16, 2, 16, 32, 768], P('enc', 'seq')
Inputs may be any that keep to these rules, and one draw needn't show every extreme that they name: `tile_ids`: for every index j of seq, the 16 slots (e, j, k) hold each tile number of that group once; tiles 2 f and 2 f + 1 are the upper and lower half of frame f of the group. partner_slot[e, j, k] = e2 * 2 + k2 where slot (e2, j, k2) holds the tile number tile_ids[e, j, k] + 1 - 2 (tile_ids[e, j, k] % 2). `token_pos`: every position occurs exactly once. Position p is owned by index p // 256 of enc+seq (enc slowest). The 256 rows of one device send at most 8 positions to any one owner, and exactly 8 to some owner.
All inputs are finite; a program needn't handle non-finite values.
Results may differ from a plain program's by a relative error of at most 0.0063.
Values may be sent and summed in bfloat16 or wider, within the bound.
A program may use at most 128 MiB of HBM per device.

v0:
```python
import functools

import itertools

import jax
import jax.numpy as jnp
import numpy as np
from jax import lax
from jax.experimental import pallas as pl
from jax.experimental.pallas import tpu as pltpu
from jax.sharding import PartitionSpec as P

C = 768
C2 = 1536
KS = 7
TH = 16
GW = 32
SLOTS = 2
ROWS = 256
N_ENC = 8
N_SEQ = 16
N_DEV = 128
CAP = 8
SLOT_ROWS = CAP * N_DEV

def orbit(o):
    turned = [o, o[2:] + o[:2], o[1:] + o[:1]]
    return [p for q in turned for p in (q, tuple(-d % 4 for d in q))]


ALL_OFFSETS = sorted(itertools.product((0, 1, 3, 2), repeat=3), key=lambda o: -sum(min(d, 4 - d) for d in o))
ORDERED = list(dict.fromkeys(p for o in ALL_OFFSETS for p in orbit(o)))


def relayed(off, f):
    return 2 in off


def first_leg(off, f):
    return tuple(way if d == 2 else 0 for d, way in zip(off, (1 + 2 * f, 3 - 2 * f, 1 + 2 * f)))


PLACES = [(o, f) for o in ORDERED for f in (0, 1) if any(o)] + [((0, 0, 0), 1), ((0, 0, 0), 0)]
DESTS = [p for p in PLACES if relayed(*p)] + [p for p in PLACES if not relayed(*p)]
N_FAR = sum(relayed(*p) for p in PLACES)
OWN = N_DEV - 1
HALF_DEV = N_DEV // 2


def packed(values):
    words = []
    for n in range(0, N_DEV, 16):
        word = sum(v << (2 * i) for i, v in enumerate(values[n : n + 16]))
        words.append(word - (1 << 32) if word >> 31 else word)
    return words


WORDS = [packed([o[axis] for o, f in DESTS]) for axis in range(3)] + [packed([f for o, f in DESTS])]
HALO = 3
CELLS = TH * GW
RIM = HALO * GW
FR, FC = TH + 2 * HALO, GW + HALO
N_FREQ = FR * (FC // 2 + 1)
HALF_F = 400
ALL_F = 2 * HALF_F
TAPS = 8 * KS
SQRT_HALF = 0.7071067811865476
INV_ROOT = 0.3989422804014327
BF = jnp.bfloat16
F32 = jnp.float32
I32 = jnp.int32


def transforms():
    kr, kc = [v.reshape(-1, 1) for v in np.meshgrid(np.arange(FR), np.arange(FC // 2 + 1), indexing="ij")]

    def wave(r, c):
        return np.exp(2j * np.pi * (kr * r / FR + kc * c / FC))

    def rows_of(z):
        out = np.zeros((ALL_F, z.shape[1]))
        out[:N_FREQ], out[HALF_F : HALF_F + N_FREQ] = z.real, z.imag
        return out

    r, c = [v.ravel() for v in np.meshgrid(np.arange(TH), np.arange(GW), indexing="ij")]
    by_patch = np.argsort(((r % 2) * 2 + c % 2) * 128 + (r // 2) * 16 + c // 2)
    rr, rc = [v.ravel() for v in np.meshgrid(np.arange(HALO), np.arange(GW), indexing="ij")]
    rim_patch = np.argsort(rr * GW + (rc % 2) * 16 + rc // 2)
    there = rows_of(np.conj(wave(r, c)))
    rims = [rows_of(np.conj(wave(rr + at, rc))) for at in (-HALO, TH)]
    rim_cells = np.concatenate(rims, axis=1)
    rim_patches = np.concatenate([m[:, rim_patch] for m in rims], axis=1)
    share = np.where(kc == 0, 1.0, 2.0) / (FR * FC)
    back = wave(r, c) * share
    back = (rows_of(np.conj(back))).T
    a, b = np.arange(TAPS) // 8, np.arange(TAPS) % 8
    taps = rows_of(wave(a - HALO, b - HALO) * (b < KS))
    high = taps.astype(BF)
    low = (taps - high.astype(np.float64)).astype(BF)
    return [
        m.astype(BF)
        for m in (there, there[:, by_patch], rim_cells, rim_patches, back[by_patch], back, high, low)
    ]


def iota(shape, axis):
    return lax.broadcasted_iota(I32, shape, axis)


def dot(a, b):
    return jnp.dot(a, b, preferred_element_type=F32)


def kernel(
    tiles_hbm, ids_ref, partner_ref, mixk_ref, mixb_ref, w_hbm, downb_ref, pos_ref, grad_hbm,
    to_f_hbm, to_b_hbm, rim_f_hbm, rim_b_hbm, from_f_hbm, from_b_hbm, tap_high, tap_low,
    llm_ref, gout_ref,
    to_f, to_b, rim_f, rim_b, from_f, from_b, taps, wave, field, edge, mg, to_patch, to_cell,
    tiles, w, grads, mixb, downb, A, slope, tok, pg, sel, hot, owner,
    msg, rmsg, gsend, grecv, grel, tsend, trecv, trel, rimf, rimb,
    lsem, msem, gsem, tsem, fsend, frecv, bsend, brecv,
):
    enc = lax.axis_index("enc")
    seq = lax.axis_index("seq")
    me = enc * N_SEQ + seq
    cy, core = enc // 2, enc % 2

    ld_tiles = pltpu.make_async_copy(tiles_hbm.at[0, 0], tiles, lsem.at[0])
    ld_grads = pltpu.make_async_copy(grad_hbm, grads, lsem.at[1])
    ld_w = pltpu.make_async_copy(w_hbm, w, lsem.at[2])
    ld_tiles.start()
    ld_grads.start()
    ld_consts = [
        pltpu.make_async_copy(src, dst, lsem.at[3 + n])
        for n, (src, dst) in enumerate(
            ((to_f_hbm, to_f), (rim_f_hbm, rim_f), (from_f_hbm, from_f), (to_b_hbm, to_b), (rim_b_hbm, rim_b), (from_b_hbm, from_b))
        )
    ]
    for n in range(3):
        ld_consts[n].start()
    ld_w.start()
    for n in range(3, 6):
        ld_consts[n].start()

    cx, cz = seq >> 2, seq & 3
    at_x = [((cx + d) & 3) * 4 for d in range(4)]
    at_y = [((cy + d) & 3) * 2 for d in range(4)]
    at_z = [(cz + d) & 3 for d in range(4)]
    at_core = [core, 1 - core]

    def device(off, f):
        dx, dy, dz = off
        return at_y[dy] + at_core[f], at_x[dx] + at_z[dz]

    others = range(OWN)
    barrier = pltpu.get_barrier_semaphore()
    for q in others:
        pl.semaphore_signal(barrier, inc=1, device_id=device(*DESTS[q]), device_id_type=pl.DeviceIdType.MESH)


    pos = pos_ref[0, 0]
    prow = jnp.concatenate([pos[0:1, :], pos[1:2, :]], axis=1)
    pcol = jnp.concatenate(
        [jnp.transpose(jnp.broadcast_to(pos[i : i + 1, :].astype(F32), (128, 128))) for i in range(2)], axis=0
    ).astype(I32)[:, 0:1]
    orow, ocol = prow // ROWS, pcol // ROWS
    lcol = pcol - ocol * ROWS
    same = jnp.broadcast_to(ocol, (ROWS, ROWS)) == jnp.broadcast_to(orow, (ROWS, ROWS))
    at0, at1 = iota((ROWS, ROWS), 0), iota((ROWS, ROWS), 1)
    rank_row = jnp.sum(jnp.where(same & (at0 < at1), 1.0, 0.0), axis=0, keepdims=True).astype(I32)
    rank_col = jnp.sum(jnp.where(same & (at1 < at0), 1.0, 0.0), axis=1, keepdims=True).astype(I32)
    slot_row = orow * CAP + rank_row
    to_owner = jnp.where(iota((N_DEV, ROWS), 0) == orow, 1.0, 0.0).astype(BF)
    ranked = jnp.where(iota((ROWS, 128), 1) == rank_col, (lcol + 1).astype(F32), 0.0).astype(BF)
    msg[...] = dot(to_owner, ranked).reshape(N_DEV, 1, 128)
    rmsg[pl.ds(me, 1)] = msg[pl.ds(me, 1)]

    def lower(k):
        return lax.rem(ids_ref[0, 0, k], 2)

    up = lax.rem(cy + 1, 4) * 2 + core
    down = lax.rem(cy + 3, 4) * 2 + core
    across = lax.rem(cy + 2, 4) * 2 + core
    sib = cy * 2 + 1 - core

    def rim_copies(rims, ssem, rsem):
        def copy(n, ref, to):
            return pltpu.make_async_remote_copy(
                src_ref=ref, dst_ref=ref, send_sem=ssem.at[n], recv_sem=rsem.at[n],
                device_id=(to, seq), device_id_type=pl.DeviceIdType.MESH,
            )

        def landed(n, ref):
            return pltpu.make_async_copy(ref, ref, rsem.at[n])

        sends = [
            copy(0, rims.at[enc], up),
            copy(1, rims.at[enc], down),
            copy(2, rims.at[enc], sib),
            copy(3, rims.at[down, 0], up),
            copy(4, rims.at[up, 1], down),
            copy(5, rims.at[down], sib),
            copy(6, rims.at[up], sib),
            copy(7, rims.at[across], sib),
        ]
        other = 1 - 2 * core
        arrivals = [
            landed(0, rims.at[down]),
            landed(1, rims.at[up]),
            landed(2, rims.at[sib]),
            landed(3, rims.at[across, 0]),
            landed(4, rims.at[across, 1]),
            landed(5, rims.at[down + other]),
            landed(6, rims.at[up + other]),
            landed(7, rims.at[across + other]),
        ]
        return sends, arrivals

    def place_rims(rims):
        for k in range(SLOTS):
            want = partner_ref[0, 0, k]
            rim = jnp.zeros((RIM, C), BF)
            for q in range(N_ENC * SLOTS):
                rim = jnp.where(want == q, rims[q // 2, q % 2], rim)
            none = jnp.zeros((RIM, C), BF)
            below = lower(k) == 1
            edge[k, 0:RIM, :] = jnp.where(below, rim, none)
            edge[k, RIM : 2 * RIM, :] = jnp.where(below, none, rim)

    def columns(n):
        return pl.ds(pl.multiple_of(n * 256, 256), 256)

    def spectrum(there, cells):
        @pl.loop(0, SLOTS * 3)
        def _(i):
            k, cols = i // 3, columns(lax.rem(i, 3))
            field[k, :, cols] = dot(there, cells(k, cols))

    def depthwise(there, back, way, turn, cells, store):
        @pl.loop(0, SLOTS * 3)
        def _(i):
            k, cols = i // 3, columns(lax.rem(i, 3))
            z = field[k, :, cols] + dot(there[...], edge[k, :, cols])
            re, im = z[0:HALF_F], z[HALF_F:ALL_F]
            wr, wi = wave[0:HALF_F, cols], way * wave[HALF_F:ALL_F, cols]
            product = jnp.concatenate([re * wr - im * wi, re * wi + im * wr], axis=0).astype(BF)
            store(k, cols, dot(turn[...], cells(k, cols)) + dot(back[...], product))

    def owner_of_row():
        place = iota((SLOT_ROWS, 1), 0) // CAP
        block, shift = place // 16, 2 * (place % 16)
        d = []
        for words in WORDS:
            word = jnp.full(place.shape, words[0])
            for n in range(1, 8):
                word = jnp.where(block == n, words[n], word)
            d.append(jnp.right_shift(word, shift) & 3)
        c = core + d[3] - 2 * core * d[3]
        return (((cy + d[1]) & 3) * 2 + c) * N_SEQ + ((cx + d[0]) & 3) * 4 + ((cz + d[2]) & 3)

    def fill_rows(buf, rows_ref, part):
        slots = slice(part * SLOT_ROWS // 2, (part + 1) * SLOT_ROWS // 2)
        dests = slice(part * HALF_DEV, (part + 1) * HALF_DEV)

        @pl.loop(0, C // 256)
        def _(n):
            c0 = pl.multiple_of(n * 256, 256)
            y0 = dot(hot[slots, :], rows_ref[:, pl.ds(c0, 256)]).reshape(HALF_DEV, CAP, 256)
            y1 = dot(hot[slots, :], rows_ref[:, pl.ds(c0 + C, 256)]).reshape(HALF_DEV, CAP, 256)
            buf[dests, :, pl.ds(c0, 256)] = jnp.concatenate([y0, y1], axis=1).astype(BF)

    def send_rows(buf, rel, got, sems, part):
        for q in others:
            if q // HALF_DEV == part:
                off, f = DESTS[q]
                far = q < N_FAR
                pltpu.make_async_remote_copy(
                    src_ref=buf.at[q], dst_ref=rel.at[q] if far else got.at[me],
                    send_sem=sems.at[0], recv_sem=sems.at[2 if far else 1],
                    device_id=device(first_leg(off, f), 0) if far else device(off, f),
                    device_id_type=pl.DeviceIdType.MESH,
                ).start()

    def forward(rel, got, sems):
        part = rel.at[pl.ds(0, N_FAR)]
        pltpu.make_async_copy(part, part, sems.at[2]).wait()
        for q in range(N_FAR):
            off, f = DESTS[q]
            leg = first_leg(off, f)
            e0, s0 = device([-d % 4 for d in leg], 0)
            pltpu.make_async_remote_copy(
                src_ref=rel.at[q], dst_ref=got.at[e0 * N_SEQ + s0],
                send_sem=sems.at[3], recv_sem=sems.at[1],
                device_id=device([(o - d) % 4 for o, d in zip(off, leg)], f), device_id_type=pl.DeviceIdType.MESH,
            ).start()

    def keep_own(buf, got):
        got[pl.ds(me, 1)] = buf[OWN : OWN + 1]

    def wait_rows(buf, sem):
        part = buf.at[pl.ds(0, N_DEV - 1)]
        pltpu.make_async_copy(part, part, sem).wait()

    ld_tiles.wait()
    for k in range(SLOTS):
        high, low = tiles[k, TH - HALO : TH].reshape(RIM, C), tiles[k, 0:HALO].reshape(RIM, C)
        rimf[enc, k] = jnp.where(lower(k) == 0, high, low)
    pl.semaphore_wait(barrier, N_DEV - 1)
    for q in others:
        e, s = device(*DESTS[q])
        pltpu.make_async_remote_copy(
            src_ref=msg.at[e * N_SEQ + s], dst_ref=rmsg.at[me],
            send_sem=msem.at[0], recv_sem=msem.at[1],
            device_id=(e, s), device_id_type=pl.DeviceIdType.MESH,
        ).start()
    f_send, f_got = rim_copies(rimf, fsend, frecv)
    for n in range(3):
        f_send[n].start()
    owner[...] = owner_of_row()

    def tile_cells(k, cols):
        return tiles[k, :, :, cols].reshape(CELLS, 256)

    def grad_cells(k, cols):
        return mg[k, :, cols]

    ld_grads.wait()
    wait_rows(rmsg, msem.at[1])

    asked = rmsg[...].reshape(N_DEV, 128)
    asked_t = jnp.transpose(asked)[0:CAP, :].astype(BF)
    asked = asked.astype(BF)

    shape = (SLOT_ROWS, 128)
    rows = dot(jnp.where(iota(shape, 1) == owner[...], 1.0, 0.0).astype(BF), asked)
    want = jnp.sum(jnp.where(iota(shape, 1) == iota(shape, 0) % CAP, rows, 0.0), axis=1, keepdims=True).astype(I32)
    hot[...] = jnp.where(iota((SLOT_ROWS, ROWS), 1) == want - 1, 1.0, 0.0).astype(BF)
    for part in range(2):
        fill_rows(gsend, grads, part)
    f_got[0].wait()
    f_send[3].start()
    f_send[5].start()
    f_got[1].wait()
    f_send[4].start()
    f_send[6].start()
    for part in range(2):
        send_rows(gsend, grel, grecv, gsem, part)
    keep_own(gsend, grecv)

    mixb[...] = mixb_ref[...].reshape(1, C)
    downb[...] = downb_ref[...].reshape(1, C2)

    def cell_of(m):
        return ((m % 128) // 16 * 2 + m // 256) * GW + m % 16 * 2 + m // 128 % 2

    p0, p1 = iota((CELLS, CELLS), 0), iota((CELLS, CELLS), 1)
    to_patch[...] = jnp.where(p1 == cell_of(p0), 1.0, 0.0).astype(BF)
    to_cell[...] = jnp.where(p0 == cell_of(p1), 1.0, 0.0).astype(BF)

    taps[...] = jnp.zeros((TAPS, C), F32)
    for a in range(KS):
        taps[8 * a : 8 * a + KS, :] = mixk_ref[a].astype(F32)
    flat_taps = taps[...].astype(BF)
    wave[...] = dot(tap_high[...], flat_taps) + dot(tap_low[...], flat_taps)

    ld_consts[0].wait()
    spectrum(to_f[...], tile_cells)
    forward(grel, grecv, gsem)
    f_got[3].wait()
    f_got[4].wait()
    f_send[7].start()
    for n in (2, 5, 6, 7):
        f_got[n].wait()
    place_rims(rimf)
    ld_consts[1].wait()
    ld_consts[2].wait()

    def store_mixed(k, cols, cells):
        mixed = (cells + mixb[:, cols]).astype(BF)
        A[:, pl.ds(pl.multiple_of(k * 128, 128), 128), cols] = mixed.reshape(4, 128, 256)

    depthwise(rim_f, from_f, 1.0, to_patch, tile_cells, store_mixed)
    ld_w.wait()

    @pl.loop(0, C2 // 256)
    def _(n):
        cols = pl.ds(pl.multiple_of(n * 256, 256), 256)
        pre = jnp.zeros((ROWS, 256), F32) + downb[:, cols]
        for j in range(4):
            pre = pre + dot(A[j], w[j * C : (j + 1) * C, cols])
        phi = 0.5 * (1.0 + lax.erf(pre * SQRT_HALF))
        tok[:, cols] = (pre * phi).astype(BF)
        slope[:, cols] = phi + pre * INV_ROOT * jnp.exp(-0.5 * pre * pre)

    at = owner[...] * CAP + iota((SLOT_ROWS, 1), 0) % CAP
    hot[...] = jnp.where(at == slot_row, 1.0, 0.0).astype(BF)
    for part in range(2):
        fill_rows(tsend, tok, part)
        send_rows(tsend, trel, trecv, tsem, part)
    keep_own(tsend, trecv)

    back_at = ocol * (2 * CAP) + rank_col
    for h in range(2):
        sel[h] = jnp.where(iota((ROWS, 2 * CAP * N_DEV), 1) == back_at + h * CAP, 1.0, 0.0).astype(BF)
    wait_rows(grecv, gsem.at[1])

    def picked(got, h, c0):
        part = got[:, :, pl.ds(pl.multiple_of(c0, 256), 256)].reshape(2 * CAP * N_DEV, 256)
        return dot(sel[h], part)

    @pl.loop(0, C2 // 256)
    def _(n):
        h = n // 3
        cols = pl.ds(pl.multiple_of(n * 256, 256), 256)
        pg[:, cols] = (picked(grecv, h, (n - 3 * h) * 256) * slope[:, cols]).astype(BF)

    forward(trel, trecv, tsem)

    @pl.loop(0, 4 * (C // 256))
    def _(m):
        j, n = m // 3, lax.rem(m, 3)
        part = w[pl.ds(pl.multiple_of(m * 256, 256), 256), :]
        g = lax.dot_general(pg[...], part, (((1,), (1,)), ((), ())), preferred_element_type=F32)
        mg[:, pl.ds(pl.multiple_of(j * 128, 128), 128), columns(n)] = g.astype(BF).reshape(SLOTS, 128, 256)

    def rim_rows(k, rows):
        at = [((r % 2) * 2 + dx) * 128 + (r // 2) * 16 for r in rows for dx in range(2)]
        return jnp.concatenate([mg[k, a : a + 16, :] for a in at], axis=0)

    for k in range(SLOTS):
        rimb[enc, k] = jnp.where(lower(k) == 0, rim_rows(k, range(TH - HALO, TH)), rim_rows(k, range(HALO)))
    b_send, b_got = rim_copies(rimb, bsend, brecv)
    for n in range(3):
        b_send[n].start()
    ld_consts[3].wait()
    spectrum(to_b[...], grad_cells)
    b_got[0].wait()
    b_send[3].start()
    b_send[5].start()
    b_got[1].wait()
    b_send[4].start()
    b_send[6].start()
    b_got[3].wait()
    b_got[4].wait()
    b_send[7].start()
    for n in (2, 5, 6, 7):
        b_got[n].wait()
    place_rims(rimb)
    ld_consts[4].wait()
    ld_consts[5].wait()

    def store_grad(k, cols, cells):
        gout_ref[k, :, :, cols] = cells.astype(BF).reshape(TH, GW, 256)

    depthwise(rim_b, from_b, -1.0, to_cell, grad_cells, store_grad)

    for g in range(N_DEV // N_SEQ):
        shape = (N_DEV, 256)
        at1 = iota(shape, 1)
        over = jnp.where(iota(shape, 0) == g * N_SEQ + at1 // (2 * CAP), 1.0, 0.0).astype(BF)
        rows = dot(asked_t, over)
        k8 = iota((CAP, 256), 1)
        put = jnp.sum(jnp.where(iota((CAP, 256), 0) == k8 % CAP, rows, 0.0), axis=0, keepdims=True).astype(I32)
        hit = iota((ROWS, 256), 0) == put - 1
        part = (iota((ROWS, 256), 1) // CAP) % 2
        for h in range(2):
            sel[h, :, g * 256 : (g + 1) * 256] = jnp.where(hit & (part == h), 1.0, 0.0).astype(BF)
    wait_rows(trecv, tsem.at[1])

    @pl.loop(0, C2 // 256)
    def _(n):
        h = n // 3
        cols = pl.ds(pl.multiple_of(n * 256, 256), 256)
        llm_ref[:, cols] = picked(trecv, h, (n - 3 * h) * 256).astype(BF)

    for n in range(8):
        f_send[n].wait_send()
        b_send[n].wait_send()
    wait_rows(msg, msem.at[0])
    for buf, rel, sems in ((gsend, grel, gsem), (tsend, trel, tsem)):
        wait_rows(buf, sems.at[0])
        part = rel.at[pl.ds(0, N_FAR)]
        pltpu.make_async_copy(part, part, sems.at[3]).wait()


def on_device(frame_tiles, tile_ids, partner_slot, mix_kernel, mix_bias, down_weight, down_bias, token_pos, grad_rows):
    vmem = pl.BlockSpec(memory_space=pltpu.VMEM)
    smem = pl.BlockSpec(memory_space=pltpu.SMEM)
    anyw = pl.BlockSpec(memory_space=pl.ANY)
    dma = pltpu.SemaphoreType.DMA
    llm, gout = pl.pallas_call(
        kernel,
        out_shape=(
            jax.ShapeDtypeStruct((ROWS, C2), BF),
            jax.ShapeDtypeStruct((SLOTS, TH, GW, C), BF),
        ),
        in_specs=[anyw, smem, smem, vmem, vmem, anyw, vmem, vmem, anyw] + [anyw] * 6 + [vmem] * 2,
        out_specs=(vmem, vmem),
        scratch_shapes=[
            pltpu.VMEM((ALL_F, CELLS), BF),
            pltpu.VMEM((ALL_F, CELLS), BF),
            pltpu.VMEM((ALL_F, 2 * RIM), BF),
            pltpu.VMEM((ALL_F, 2 * RIM), BF),
            pltpu.VMEM((CELLS, ALL_F), BF),
            pltpu.VMEM((CELLS, ALL_F), BF),
            pltpu.VMEM((TAPS, C), F32),
            pltpu.VMEM((ALL_F, C), F32),
            pltpu.VMEM((SLOTS, ALL_F, C), F32),
            pltpu.VMEM((SLOTS, 2 * RIM, C), BF),
            pltpu.VMEM((SLOTS, CELLS, C), BF),
            pltpu.VMEM((CELLS, CELLS), BF),
            pltpu.VMEM((CELLS, CELLS), BF),
            pltpu.VMEM((SLOTS, TH, GW, C), BF),
            pltpu.VMEM((4 * C, C2), BF),
            pltpu.VMEM((ROWS, C2), BF),
            pltpu.VMEM((1, C), F32),
            pltpu.VMEM((1, C2), F32),
            pltpu.VMEM((4, ROWS, C), BF),
            pltpu.VMEM((ROWS, C2), F32),
            pltpu.VMEM((ROWS, C2), BF),
            pltpu.VMEM((ROWS, C2), BF),
            pltpu.VMEM((2, ROWS, 2 * CAP * N_DEV), BF),
            pltpu.VMEM((SLOT_ROWS, ROWS), BF),
            pltpu.VMEM((SLOT_ROWS, 1), I32),
            pltpu.VMEM((N_DEV, 1, 128), F32),
            pltpu.VMEM((N_DEV, 1, 128), F32),
            pltpu.VMEM((N_DEV, 2 * CAP, C), BF),
            pltpu.VMEM((N_DEV, 2 * CAP, C), BF),
            pltpu.VMEM((N_FAR, 2 * CAP, C), BF),
            pltpu.VMEM((N_DEV, 2 * CAP, C), BF),
            pltpu.VMEM((N_DEV, 2 * CAP, C), BF),
            pltpu.VMEM((N_FAR, 2 * CAP, C), BF),
            pltpu.VMEM((N_ENC, SLOTS, RIM, C), BF),
            pltpu.VMEM((N_ENC, SLOTS, RIM, C), BF),
            dma((9,)),
            dma((2,)),
            dma((4,)),
            dma((4,)),
            dma((8,)),
            dma((8,)),
            dma((8,)),
            dma((8,)),
        ],
        compiler_params=pltpu.CompilerParams(
            collective_id=0, has_side_effects=True, vmem_limit_bytes=62 * 1024 * 1024
        ),
    )(
        frame_tiles,
        tile_ids,
        partner_slot,
        mix_kernel,
        mix_bias,
        down_weight,
        down_bias,
        token_pos,
        grad_rows,
        *transforms(),
    )
    return llm, gout[None, None]


def solution(mesh):
    return jax.shard_map(
        on_device,
        mesh=mesh,
        in_specs=(
            P("enc", "seq", None, None, None, None),
            P("enc", "seq", None),
            P("enc", "seq", None),
            P(),
            P(),
            P(),
            P(),
            P("enc", "seq", None, None),
            P(("enc", "seq"), None),
        ),
        out_specs=(P(("enc", "seq"), None), P("enc", "seq", None, None, None, None)),
        check_vma=False,
    )
```

profile of v0, /device:TPU:1, one launch (start us, length us, event | category | flops | bytes accessed | tf_op | source)
XLA Modules:
  0.0 122.3 jit_solution(1688204382022945073)
XLA Ops:
  0.6 118.3 %shard_map.176 = (bf16[256,1536]{1,0:T(8,128)(2,1)}, bf16[2,16,32,768]{3,2,1,0:T(8,128)(2,1)}) custom-call(bf16[1,1,2,16,32,768]{5,4,3,2,1,0:T(8,128)(2,1)} %tiles_hbm.1, s32[1,1,2]{2,1,0:T(1,128)} %ids_ref.1, s32[1,1,2]{2,1,0:T(1,128)} %partner_ref.1, bf16[7,7,768]{2,1,0:T(8,128)(2,1)} %mixk_ref.1, f32[768]{0:T(1024)} %mixb_ref.1, ...), custom_call_target="tpu_custom_call" | custom-call | tf_op jit(solution)/shard_map/pallas_call | solution.py:491
  119.0 0.0 copy-start
  119.0 2.2 %copy.21 = bf16[256,1536]{1,0:T(8,128)(2,1)} copy(bf16[256,1536]{1,0:T(8,128)(2,1)} %get-tuple-element.8) | data formatting | bytes 1572864
  121.2 0.0 copy-done
  121.2 1.1 copy.22
Async XLA Ops:
  119.0 2.2 %copy-start = (bf16[2,16,32,768]{3,2,1,0:T(8,128)(2,1)S(1)}, bf16[2,16,32,768]{3,2,1,0:T(8,128)(2,1)}, u32[]{:S(2)}) copy-start(bf16[2,16,32,768]{3,2,1,0:T(8,128)(2,1)} %get-tuple-element.5) | copy-start | bytes 4718596
where the time goes:
time: 122 us
  Pallas kernels  118 us (97%)
  local copies, waits for them, and re-layouts  3.33 us (3%)
    pallas_call x1, Pallas kernels, on_device(): pl.pallas_call(kernel, out_shape=(jax.ShapeDtypeStruct((ROWS, C2), BF), j...  118 us
    unnamed x4, local copies, waits for them, and re-layouts  3.33 us

commit v1 on v0

--- a/solution.py
+++ b/solution.py
@@ -114,8 +114,8 @@
 def kernel(
     tiles_hbm, ids_ref, partner_ref, mixk_ref, mixb_ref, w_hbm, downb_ref, pos_ref, grad_hbm,
     to_f_hbm, to_b_hbm, rim_f_hbm, rim_b_hbm, from_f_hbm, from_b_hbm, tap_high, tap_low,
-    llm_ref, gout_ref,
-    to_f, to_b, rim_f, rim_b, from_f, from_b, taps, wave, field, edge, mg, to_patch, to_cell,
+    llm_hbm, gout_hbm,
+    to_f, to_b, rim_f, rim_b, from_f, from_b, taps, wave, field, edge, mg, to_patch, to_cell, llm_ref, gout_ref, osem,
     tiles, w, grads, mixb, downb, A, slope, tok, pg, sel, hot, owner,
     msg, rmsg, gsend, grecv, grel, tsend, trecv, trel, rimf, rimb,
     lsem, msem, gsem, tsem, fsend, frecv, bsend, brecv,
@@ -269,17 +269,16 @@
             y1 = dot(hot[slots, :], rows_ref[:, pl.ds(c0 + C, 256)]).reshape(HALF_DEV, CAP, 256)
             buf[dests, :, pl.ds(c0, 256)] = jnp.concatenate([y0, y1], axis=1).astype(BF)
 
-    def send_rows(buf, rel, got, sems, part):
-        for q in others:
-            if q // HALF_DEV == part:
-                off, f = DESTS[q]
-                far = q < N_FAR
-                pltpu.make_async_remote_copy(
-                    src_ref=buf.at[q], dst_ref=rel.at[q] if far else got.at[me],
-                    send_sem=sems.at[0], recv_sem=sems.at[2 if far else 1],
-                    device_id=device(first_leg(off, f), 0) if far else device(off, f),
-                    device_id_type=pl.DeviceIdType.MESH,
-                ).start()
+    def send_rows(buf, rel, got, sems, chosen):
+        for q in chosen:
+            off, f = DESTS[q]
+            far = q < N_FAR
+            pltpu.make_async_remote_copy(
+                src_ref=buf.at[q], dst_ref=rel.at[q] if far else got.at[me],
+                send_sem=sems.at[0], recv_sem=sems.at[2 if far else 1],
+                device_id=device(first_leg(off, f), 0) if far else device(off, f),
+                device_id_type=pl.DeviceIdType.MESH,
+            ).start()
 
     def forward(rel, got, sems):
         part = rel.at[pl.ds(0, N_FAR)]
@@ -337,14 +336,14 @@
     hot[...] = jnp.where(iota((SLOT_ROWS, ROWS), 1) == want - 1, 1.0, 0.0).astype(BF)
     for part in range(2):
         fill_rows(gsend, grads, part)
+    send_rows(gsend, grel, grecv, gsem, [q for q in others if DESTS[q][0][1] == 0])
     f_got[0].wait()
     f_send[3].start()
     f_send[5].start()
     f_got[1].wait()
     f_send[4].start()
     f_send[6].start()
-    for part in range(2):
-        send_rows(gsend, grel, grecv, gsem, part)
+    send_rows(gsend, grel, grecv, gsem, [q for q in others if DESTS[q][0][1] != 0])
     keep_own(gsend, grecv)
 
     mixb[...] = mixb_ref[...].reshape(1, C)
@@ -396,7 +395,7 @@
     hot[...] = jnp.where(at == slot_row, 1.0, 0.0).astype(BF)
     for part in range(2):
         fill_rows(tsend, tok, part)
-        send_rows(tsend, trel, trecv, tsem, part)
+        send_rows(tsend, trel, trecv, tsem, others[part * HALF_DEV : (part + 1) * HALF_DEV])
     keep_own(tsend, trecv)
 
     back_at = ocol * (2 * CAP) + rank_col
@@ -413,8 +412,6 @@
         h = n // 3
         cols = pl.ds(pl.multiple_of(n * 256, 256), 256)
         pg[:, cols] = (picked(grecv, h, (n - 3 * h) * 256) * slope[:, cols]).astype(BF)
-
-    forward(trel, trecv, tsem)
 
     @pl.loop(0, 4 * (C // 256))
     def _(m):
@@ -432,6 +429,7 @@
     b_send, b_got = rim_copies(rimb, bsend, brecv)
     for n in range(3):
         b_send[n].start()
+    forward(trel, trecv, tsem)
     ld_consts[3].wait()
     spectrum(to_b[...], grad_cells)
     b_got[0].wait()
@@ -453,6 +451,8 @@
         gout_ref[k, :, :, cols] = cells.astype(BF).reshape(TH, GW, 256)
 
     depthwise(rim_b, from_b, -1.0, to_cell, grad_cells, store_grad)
+    put_gout = pltpu.make_async_copy(gout_ref, gout_hbm, osem.at[6])
+    put_gout.start()
 
     for g in range(N_DEV // N_SEQ):
         shape = (N_DEV, 256)
@@ -472,7 +472,12 @@
         h = n // 3
         cols = pl.ds(pl.multiple_of(n * 256, 256), 256)
         llm_ref[:, cols] = picked(trecv, h, (n - 3 * h) * 256).astype(BF)
-
+        pltpu.make_async_copy(llm_ref.at[:, cols], llm_hbm.at[:, cols], osem.at[n]).start()
+
+    for n in range(C2 // 256):
+        cols = pl.ds(n * 256, 256)
+        pltpu.make_async_copy(llm_ref.at[:, cols], llm_hbm.at[:, cols], osem.at[n]).wait()
+    put_gout.wait()
     for n in range(8):
         f_send[n].wait_send()
         b_send[n].wait_send()
@@ -495,7 +500,7 @@
             jax.ShapeDtypeStruct((SLOTS, TH, GW, C), BF),
         ),
         in_specs=[anyw, smem, smem, vmem, vmem, anyw, vmem, vmem, anyw] + [anyw] * 6 + [vmem] * 2,
-        out_specs=(vmem, vmem),
+        out_specs=(anyw, anyw),
         scratch_shapes=[
             pltpu.VMEM((ALL_F, CELLS), BF),
             pltpu.VMEM((ALL_F, CELLS), BF),
@@ -510,6 +515,9 @@
             pltpu.VMEM((SLOTS, CELLS, C), BF),
             pltpu.VMEM((CELLS, CELLS), BF),
             pltpu.VMEM((CELLS, CELLS), BF),
+            pltpu.VMEM((ROWS, C2), BF),
+            pltpu.VMEM((SLOTS, TH, GW, C), BF),
+            dma((7,)),
             pltpu.VMEM((SLOTS, TH, GW, C), BF),
             pltpu.VMEM((4 * C, C2), BF),
             pltpu.VMEM((ROWS, C2), BF),

time: 122 us -> 122 us (level)
  the two profiles are of different devices: /device:TPU:1 before, /device:TPU:69 now
where the time goes in v1:
time: 122 us
  Pallas kernels  118 us (97%)
  local copies, waits for them, and re-layouts  3.33 us (3%)
    pallas_call x1, Pallas kernels, on_device(): pl.pallas_call(kernel, out_shape=(jax.ShapeDtypeStruct((ROWS, C2), BF), j...  118 us
    unnamed x4, local copies, waits for them, and re-layouts  3.33 us

profile of v1, /device:TPU:69, one launch (start us, length us, event | category | flops | bytes accessed | tf_op | source)
XLA Modules:
  0.0 121.9 jit_solution(13534633530605656422)
XLA Ops:
  0.6 117.9 %shard_map.176 = (bf16[256,1536]{1,0:T(8,128)(2,1)}, bf16[2,16,32,768]{3,2,1,0:T(8,128)(2,1)}) custom-call(bf16[1,1,2,16,32,768]{5,4,3,2,1,0:T(8,128)(2,1)} %tiles_hbm.1, s32[1,1,2]{2,1,0:T(1,128)} %ids_ref.1, s32[1,1,2]{2,1,0:T(1,128)} %partner_ref.1, bf16[7,7,768]{2,1,0:T(8,128)(2,1)} %mixk_ref.1, f32[768]{0:T(1024)} %mixb_ref.1, ...), custom_call_target="tpu_custom_call" | custom-call | tf_op jit(solution)/shard_map/pallas_call | solution.py:496
  118.6 0.0 copy-start
  118.6 2.2 %copy.21 = bf16[256,1536]{1,0:T(8,128)(2,1)} copy(bf16[256,1536]{1,0:T(8,128)(2,1)} %get-tuple-element.8) | data formatting | bytes 1572864
  120.7 0.0 copy-done
  120.8 1.1 copy.22
Async XLA Ops:
  118.6 2.2 %copy-start = (bf16[2,16,32,768]{3,2,1,0:T(8,128)(2,1)S(1)}, bf16[2,16,32,768]{3,2,1,0:T(8,128)(2,1)}, u32[]{:S(2)}) copy-start(bf16[2,16,32,768]{3,2,1,0:T(8,128)(2,1)} %get-tuple-element.5) | copy-start | bytes 4718596

commit v2 on v1

--- a/solution.py
+++ b/solution.py
@@ -395,7 +395,9 @@
     hot[...] = jnp.where(at == slot_row, 1.0, 0.0).astype(BF)
     for part in range(2):
         fill_rows(tsend, tok, part)
-        send_rows(tsend, trel, trecv, tsem, others[part * HALF_DEV : (part + 1) * HALF_DEV])
+        if part == 0:
+            send_rows(tsend, trel, trecv, tsem, others[:HALF_DEV])
+    send_rows(tsend, trel, trecv, tsem, others[HALF_DEV:N_FAR])
     keep_own(tsend, trecv)
 
     back_at = ocol * (2 * CAP) + rank_col
@@ -432,27 +434,6 @@
     forward(trel, trecv, tsem)
     ld_consts[3].wait()
     spectrum(to_b[...], grad_cells)
-    b_got[0].wait()
-    b_send[3].start()
-    b_send[5].start()
-    b_got[1].wait()
-    b_send[4].start()
-    b_send[6].start()
-    b_got[3].wait()
-    b_got[4].wait()
-    b_send[7].start()
-    for n in (2, 5, 6, 7):
-        b_got[n].wait()
-    place_rims(rimb)
-    ld_consts[4].wait()
-    ld_consts[5].wait()
-
-    def store_grad(k, cols, cells):
-        gout_ref[k, :, :, cols] = cells.astype(BF).reshape(TH, GW, 256)
-
-    depthwise(rim_b, from_b, -1.0, to_cell, grad_cells, store_grad)
-    put_gout = pltpu.make_async_copy(gout_ref, gout_hbm, osem.at[6])
-    put_gout.start()
 
     for g in range(N_DEV // N_SEQ):
         shape = (N_DEV, 256)
@@ -465,6 +446,30 @@
         part = (iota((ROWS, 256), 1) // CAP) % 2
         for h in range(2):
             sel[h, :, g * 256 : (g + 1) * 256] = jnp.where(hit & (part == h), 1.0, 0.0).astype(BF)
+
+    b_got[0].wait()
+    b_send[3].start()
+    b_send[5].start()
+    b_got[1].wait()
+    b_send[4].start()
+    b_send[6].start()
+    send_rows(tsend, trel, trecv, tsem, others[N_FAR:])
+    b_got[3].wait()
+    b_got[4].wait()
+    b_send[7].start()
+    for n in (2, 5, 6, 7):
+        b_got[n].wait()
+    place_rims(rimb)
+    ld_consts[4].wait()
+    ld_consts[5].wait()
+
+    def store_grad(k, cols, cells):
+        gout_ref[k, :, :, cols] = cells.astype(BF).reshape(TH, GW, 256)
+
+    depthwise(rim_b, from_b, -1.0, to_cell, grad_cells, store_grad)
+    put_gout = pltpu.make_async_copy(gout_ref, gout_hbm, osem.at[6])
+    put_gout.start()
+
     wait_rows(trecv, tsem.at[1])
 
     @pl.loop(0, C2 // 256)

time: 122 us -> 121 us (level)
  the two profiles are of different devices: /device:TPU:69 before, /device:TPU:1 now
where the time goes in v2:
time: 121 us; the launch traced here: 120 us
  Pallas kernels  116 us (96%)
  local copies, waits for them, and re-layouts  3.33 us (3%)
    pallas_call x1, Pallas kernels, on_device(): pl.pallas_call(kernel, out_shape=(jax.ShapeDtypeStruct((ROWS, C2), BF), j...  116 us
    unnamed x4, local copies, waits for them, and re-layouts  3.33 us

profile of v2, /device:TPU:1, one launch (start us, length us, event | category | flops | bytes accessed | tf_op | source)
XLA Modules:
  0.0 120.0 jit_solution(6367730603532924083)
XLA Ops:
  0.6 116.1 %shard_map.176 = (bf16[256,1536]{1,0:T(8,128)(2,1)}, bf16[2,16,32,768]{3,2,1,0:T(8,128)(2,1)}) custom-call(bf16[1,1,2,16,32,768]{5,4,3,2,1,0:T(8,128)(2,1)} %tiles_hbm.1, s32[1,1,2]{2,1,0:T(1,128)} %ids_ref.1, s32[1,1,2]{2,1,0:T(1,128)} %partner_ref.1, bf16[7,7,768]{2,1,0:T(8,128)(2,1)} %mixk_ref.1, f32[768]{0:T(1024)} %mixb_ref.1, ...), custom_call_target="tpu_custom_call" | custom-call | tf_op jit(solution)/shard_map/pallas_call | solution.py:501
  116.7 0.0 copy-start
  116.7 2.2 %copy.21 = bf16[256,1536]{1,0:T(8,128)(2,1)} copy(bf16[256,1536]{1,0:T(8,128)(2,1)} %get-tuple-element.8) | data formatting | bytes 1572864
  118.9 0.0 copy-done
  118.9 1.1 copy.22
Async XLA Ops:
  116.7 2.2 %copy-start = (bf16[2,16,32,768]{3,2,1,0:T(8,128)(2,1)S(1)}, bf16[2,16,32,768]{3,2,1,0:T(8,128)(2,1)}, u32[]{:S(2)}) copy-start(bf16[2,16,32,768]{3,2,1,0:T(8,128)(2,1)} %get-tuple-element.5) | copy-start | bytes 4718596

commit v3 on v2

--- a/solution.py
+++ b/solution.py
@@ -491,6 +491,20 @@
         wait_rows(buf, sems.at[0])
         part = rel.at[pl.ds(0, N_FAR)]
         pltpu.make_async_copy(part, part, sems.at[3]).wait()
+
+
+def hand_over(llm_ref, gout_ref, llm_out, gout_out, sems):
+    copies = [
+        pltpu.make_async_copy(llm_ref.at[pl.ds(n * 128, 128)], llm_out.at[pl.ds(n * 128, 128)], sems.at[n])
+        for n in range(2)
+    ] + [
+        pltpu.make_async_copy(gout_ref.at[n // 2, pl.ds(n % 2 * 8, 8)], gout_out.at[n // 2, pl.ds(n % 2 * 8, 8)], sems.at[2 + n])
+        for n in range(4)
+    ]
+    for copy in copies:
+        copy.start()
+    for copy in copies:
+        copy.wait()
 
 
 def on_device(frame_tiles, tile_ids, partner_slot, mix_kernel, mix_bias, down_weight, down_bias, token_pos, grad_rows):
@@ -569,6 +583,16 @@
         grad_rows,
         *transforms(),
     )
+    llm, gout = pl.pallas_call(
+        hand_over,
+        out_shape=(
+            jax.ShapeDtypeStruct((ROWS, C2), BF),
+            jax.ShapeDtypeStruct((SLOTS, TH, GW, C), BF),
+        ),
+        in_specs=[vmem, vmem],
+        out_specs=(anyw, anyw),
+        scratch_shapes=[dma((6,))],
+    )(llm, gout)
     return llm, gout[None, None]
 
 

time: 121 us -> 120 us (level)
  local copies, waits for them, and re-layouts: 3.33 us -> 0 us
  Pallas kernels: 116 us -> 119 us
    unnamed x4 -> x0, local copies, waits for them, and re-layouts: 3.33 us -> none
    pallas_call x0 -> x1, Pallas kernels: none -> 3.1 us  [on_device(): pl.pallas_call(hand_over, out_shape=(jax.ShapeDtypeStruct((ROWS, C2), BF)...]
where the time goes in v3:
time: 120 us
  Pallas kernels  119 us (99%)
    pallas_call x1, Pallas kernels, on_device(): pl.pallas_call(kernel, out_shape=(jax.ShapeDtypeStruct((ROWS, C2), BF), j...  116 us
    pallas_call x1, Pallas kernels, on_device(): pl.pallas_call(hand_over, out_shape=(jax.ShapeDtypeStruct((ROWS, C2), BF)...  3.1 us

profile of v3, /device:TPU:1, one launch (start us, length us, event | category | flops | bytes accessed | tf_op | source)
XLA Modules:
  0.0 120.0 jit_solution(1078733890237935147)
XLA Ops:
  0.6 116.1 %shard_map.176 = (bf16[256,1536]{1,0:T(8,128)(2,1)}, bf16[2,16,32,768]{3,2,1,0:T(8,128)(2,1)}) custom-call(bf16[1,1,2,16,32,768]{5,4,3,2,1,0:T(8,128)(2,1)} %tiles_hbm.1, s32[1,1,2]{2,1,0:T(1,128)} %ids_ref.1, s32[1,1,2]{2,1,0:T(1,128)} %partner_ref.1, bf16[7,7,768]{2,1,0:T(8,128)(2,1)} %mixk_ref.1, f32[768]{0:T(1024)} %mixb_ref.1, ...), custom_call_target="tpu_custom_call" | custom-call | tf_op jit(solution)/shard_map/pallas_call | solution.py:515
  116.7 3.1 %shard_map.177 = (bf16[256,1536]{1,0:T(8,128)(2,1)}, bf16[2,16,32,768]{3,2,1,0:T(8,128)(2,1)}) custom-call(bf16[256,1536]{1,0:T(8,128)(2,1)} %get-tuple-element.6.llm_ref, bf16[2,16,32,768]{3,2,1,0:T(8,128)(2,1)} %get-tuple-element.7.gout_ref), custom_call_target="tpu_custom_call" | custom-call | tf_op jit(solution)/shard_map/pallas_call | solution.py:586

commit v4 on v3

--- a/solution.py
+++ b/solution.py
@@ -323,6 +323,22 @@
     def grad_cells(k, cols):
         return mg[k, :, cols]
 
+    mixb[...] = mixb_ref[...].reshape(1, C)
+    downb[...] = downb_ref[...].reshape(1, C2)
+
+    def cell_of(m):
+        return ((m % 128) // 16 * 2 + m // 256) * GW + m % 16 * 2 + m // 128 % 2
+
+    p0, p1 = iota((CELLS, CELLS), 0), iota((CELLS, CELLS), 1)
+    to_patch[...] = jnp.where(p1 == cell_of(p0), 1.0, 0.0).astype(BF)
+    to_cell[...] = jnp.where(p0 == cell_of(p1), 1.0, 0.0).astype(BF)
+
+    taps[...] = jnp.zeros((TAPS, C), F32)
+    for a in range(KS):
+        taps[8 * a : 8 * a + KS, :] = mixk_ref[a].astype(F32)
+    flat_taps = taps[...].astype(BF)
+    wave[...] = dot(tap_high[...], flat_taps) + dot(tap_low[...], flat_taps)
+
     ld_grads.wait()
     wait_rows(rmsg, msem.at[1])
 
@@ -345,22 +361,6 @@
     f_send[6].start()
     send_rows(gsend, grel, grecv, gsem, [q for q in others if DESTS[q][0][1] != 0])
     keep_own(gsend, grecv)
-
-    mixb[...] = mixb_ref[...].reshape(1, C)
-    downb[...] = downb_ref[...].reshape(1, C2)
-
-    def cell_of(m):
-        return ((m % 128) // 16 * 2 + m // 256) * GW + m % 16 * 2 + m // 128 % 2
-
-    p0, p1 = iota((CELLS, CELLS), 0), iota((CELLS, CELLS), 1)
-    to_patch[...] = jnp.where(p1 == cell_of(p0), 1.0, 0.0).astype(BF)
-    to_cell[...] = jnp.where(p0 == cell_of(p1), 1.0, 0.0).astype(BF)
-
-    taps[...] = jnp.zeros((TAPS, C), F32)
-    for a in range(KS):
-        taps[8 * a : 8 * a + KS, :] = mixk_ref[a].astype(F32)
-    flat_taps = taps[...].astype(BF)
-    wave[...] = dot(tap_high[...], flat_taps) + dot(tap_low[...], flat_taps)
 
     ld_consts[0].wait()
     spectrum(to_f[...], tile_cells)

time: 120 us -> 121 us (level)
  no operation moved by 1% of the time
where the time goes in v4:
time: 121 us
  Pallas kernels  120 us (99%)
    pallas_call x1, Pallas kernels, on_device(): pl.pallas_call(kernel, out_shape=(jax.ShapeDtypeStruct((ROWS, C2), BF), j...  117 us
    pallas_call x1, Pallas kernels, on_device(): pl.pallas_call(hand_over, out_shape=(jax.ShapeDtypeStruct((ROWS, C2), BF)...  3.1 us

profile of v4, /device:TPU:1, one launch (start us, length us, event | category | flops | bytes accessed | tf_op | source)
XLA Modules:
  0.0 121.1 jit_solution(5406463820783621575)
XLA Ops:
  0.6 117.2 %shard_map.176 = (bf16[256,1536]{1,0:T(8,128)(2,1)}, bf16[2,16,32,768]{3,2,1,0:T(8,128)(2,1)}) custom-call(bf16[1,1,2,16,32,768]{5,4,3,2,1,0:T(8,128)(2,1)} %tiles_hbm.1, s32[1,1,2]{2,1,0:T(1,128)} %ids_ref.1, s32[1,1,2]{2,1,0:T(1,128)} %partner_ref.1, bf16[7,7,768]{2,1,0:T(8,128)(2,1)} %mixk_ref.1, f32[768]{0:T(1024)} %mixb_ref.1, ...), custom_call_target="tpu_custom_call" | custom-call | tf_op jit(solution)/shard_map/pallas_call | solution.py:515
  117.8 3.1 %shard_map.177 = (bf16[256,1536]{1,0:T(8,128)(2,1)}, bf16[2,16,32,768]{3,2,1,0:T(8,128)(2,1)}) custom-call(bf16[256,1536]{1,0:T(8,128)(2,1)} %get-tuple-element.6.llm_ref, bf16[2,16,32,768]{3,2,1,0:T(8,128)(2,1)} %get-tuple-element.7.gout_ref), custom_call_target="tpu_custom_call" | custom-call | tf_op jit(solution)/shard_map/pallas_call | solution.py:586
